TPU v7x, 128 devices: a whole 4x4x4 slice. The times are simulated.
128 devices in a mesh: rep: 32 (over x, y, core), mp: 4 (over z).
Axes of the slice: x: 4, y: 4, z: 4, core: 2. Of those that a mesh axis runs over, the one named last changes fastest.
Arguments:
- tokens: bfloat16 [16384, 8192], P('rep', 'mp'), may hold values from -6 to 6
- tok_adapter: int32 [16384], P('rep'), may hold values from 0 to 255, as said below
- requests: int32 [32, 32], P('rep'), may hold values from 0 to 255, as said below
- owner_table: int32 [256], replicated, may hold values from 0 to 255, as said below
- q_weight: bfloat16 [8192, 4096], P(None, 'mp'), may hold values from -0.0625 to 0.0625
- pool_a: bfloat16 [256, 64, 8192], P('rep', None, 'mp'), may hold values from -0.0625 to 0.0625
- pool_b: bfloat16 [256, 64, 4096], P('rep', None, 'mp'), may hold values from -0.75 to 0.75
Outputs:
- queries: bfloat16 [16384, 4096], P('rep', 'mp')
Inputs may be any that keep to these rules, and one draw needn't show every extreme that they name: owner_table is a permutation of the pool rows; the owner of pool row p is the replica index p // 8. `requests`: each replica's list holds 32 distinct adapter ids; at most 2 of them lie on any one owner, and in every list some owners hold exactly 2. `tok_adapter`: each token's adapter id is one of its own replica's requested ids, and every requested id is named by some token of that replica; at most 62 tokens of one replica name adapters held by one owner, and in every replica some owner gets exactly 62.
All inputs are finite; a program needn't handle non-finite values.
Results may differ from a plain program's by a relative error of at most 0.0039.
Values may be sent and summed in bfloat16 or wider, within the bound.
A program may use at most 256 MiB of HBM per device.

v0:
```python
import jax
import jax.numpy as jnp
from jax import lax
from jax.sharding import PartitionSpec as P

CAP = 2


def per_device(tokens, tok_adapter, requests, owner_table, q_weight, pool_a, pool_b):
    rep_count = lax.axis_size("rep")
    own_index = lax.axis_index("rep")
    adp_local = pool_a.shape[0]
    rank_width = pool_a.shape[1]
    width_part = pool_a.shape[2]
    out_part = pool_b.shape[2]
    req_count = requests.shape[1]
    tok_count = tokens.shape[0]
    full_rows = lax.all_gather(tokens, "mp", axis=1, tiled=True)
    base_out = jnp.dot(full_rows, q_weight, preferred_element_type=jnp.float32)
    all_lists = lax.all_gather(requests, "rep", axis=0, tiled=True)
    pool_rows = owner_table[all_lists]
    owners = pool_rows // adp_local
    local_rows = pool_rows - owners * adp_local
    slot_ids = jnp.arange(req_count, dtype=jnp.int32)
    earlier = slot_ids[None, :] < slot_ids[:, None]
    same_owner = owners[:, :, None] == owners[:, None, :]
    slot_rank = jnp.sum((same_owner & earlier[None, :, :]).astype(jnp.int32), axis=2)
    cap_slots = jnp.arange(CAP, dtype=jnp.int32)
    row_ids = jnp.arange(adp_local, dtype=jnp.int32)
    keep_mask = ((owners == own_index)[:, :, None] & (slot_rank[:, :, None] == cap_slots)).astype(
        jnp.float32
    )
    row_match = (local_rows[:, :, None] == row_ids).astype(jnp.float32)
    select = jnp.einsum("qsk,qsj->qkj", keep_mask, row_match).astype(jnp.bfloat16)
    send_a = jnp.einsum("qkj,jrd->qkrd", select, pool_a, preferred_element_type=jnp.float32).astype(
        jnp.bfloat16
    )
    send_b = jnp.einsum("qkj,jrd->qkrd", select, pool_b, preferred_element_type=jnp.float32).astype(
        jnp.bfloat16
    )
    got_a, got_b = (
        lax.all_to_all(send_a, "rep", split_axis=0, concat_axis=0, tiled=True),
        lax.all_to_all(send_b, "rep", split_axis=0, concat_axis=0, tiled=True),
    )
    own_owner = lax.dynamic_index_in_dim(owners, own_index, 0, keepdims=False)
    own_rank = lax.dynamic_index_in_dim(slot_rank, own_index, 0, keepdims=False)
    owner_ids = jnp.arange(rep_count, dtype=jnp.int32)
    pick_slot = (own_owner[:, None, None] == owner_ids[None, :, None]) & (
        own_rank[:, None, None] == cap_slots[None, None, :]
    )
    pick_slot = pick_slot.reshape(req_count, rep_count * CAP).astype(jnp.bfloat16)
    slot_a = jnp.einsum(
        "sm,mrd->srd",
        pick_slot,
        got_a.reshape(rep_count * CAP, rank_width, width_part),
        preferred_element_type=jnp.float32,
    ).astype(jnp.bfloat16)
    slot_b = jnp.einsum(
        "sm,mrd->srd",
        pick_slot,
        got_b.reshape(rep_count * CAP, rank_width, out_part),
        preferred_element_type=jnp.float32,
    ).astype(jnp.bfloat16)
    one_hot = (tok_adapter[:, None] == requests[0][None, :]).astype(jnp.float32)
    flat_a = slot_a.reshape(req_count * rank_width, width_part)
    shrink = lax.dot_general(
        tokens, flat_a, (((1,), (1,)), ((), ())), preferred_element_type=jnp.float32
    )
    shrink = shrink.reshape(tok_count, req_count, rank_width)
    partial_rank = jnp.sum(shrink * one_hot[:, :, None], axis=1)
    rank_vals = lax.psum(partial_rank, "mp").astype(jnp.bfloat16)
    spread = (one_hot.astype(jnp.bfloat16)[:, :, None] * rank_vals[:, None, :]).reshape(
        tok_count, req_count * rank_width
    )
    delta = jnp.dot(
        spread, slot_b.reshape(req_count * rank_width, out_part), preferred_element_type=jnp.float32
    )
    return (base_out + delta).astype(jnp.bfloat16)


def solution(mesh):
    in_specs = (
        P("rep", "mp"),
        P("rep"),
        P("rep", None),
        P(),
        P(None, "mp"),
        P("rep", None, "mp"),
        P("rep", None, "mp"),
    )
    out_specs = P("rep", "mp")
    return jax.shard_map(
        per_device, mesh=mesh, in_specs=in_specs, out_specs=out_specs, check_vma=False
    )
```

profile of v0, /device:TPU:12, one launch (start us, length us, event | category | flops | bytes accessed | tf_op | source)
XLA Modules:
  0.0 548.6 jit_solution(1908256858202556166)
XLA Ops:
  6.5 0.0 copy-start
  6.6 20.8 %all-gather = s32[32,1,32]{2,1,0:T(1,128)S(1)} all-gather(s32[1,1,32]{2,1,0:T(1,128)} %bitcast.45), channel_id=1, replica_groups=mesh['rep'=32,'mp'=4] {'rep'}, dimensions={0}, use_global_device_ids=true | all-gather | bytes 4224 | tf_op jit(solution)/shard_map/all_gather | solution.py:20
  27.4 0.1 reshape.181
  27.5 0.0 copy-done.2
  27.5 6.8 %gather_fusion = s32[1024]{0:T(1024)S(1)} fusion(s32[256]{0:T(256)S(1)} %copy-done.2, s32[1024]{0:T(1024)S(1)} %broadcast_clamp_fusion), kind=kCustom, calls=%fused_computation | custom fusion | bytes 12288 | tf_op jit(solution)/shard_map/gather | solution.py:21
  34.3 0.1 reshape.180
  34.4 0.8 convert_reduce_fusion
  35.2 0.2 fusion.17
  35.4 0.1 copy.38
  35.5 0.0 copy-done.4
  35.5 4.7 convolution_convert_fusion.1
  40.2 11.3 %copy.44 = bf16[32,2,64,1024]{3,2,1,0:T(8,128)(2,1)} copy(bf16[32,2,64,1024]{3,0,2,1:T(8,128)(2,1)} %convolution_convert_fusion.1) | data formatting | bytes 16777216 | tf_op jit(solution)/shard_map/convert_element_type | solution.py:38
  51.4 6.8 %all-to-all-start.1 = ((bf16[32,2,64,1024]{3,2,1,0:T(8,128)(2,1)}), bf16[32,2,64,1024]{3,2,1,0:T(8,128)(2,1)}, u32[]{:S(2)}, u32[]{:S(2)}) async-start(bf16[32,2,64,1024]{3,2,1,0:T(8,128)(2,1)} %copy.44), calls=%async_computation.1 | async-start | bytes 16777216 | tf_op jit(solution)/shard_map/all_to_all | solution.py:43
  58.3 4.8 convolution_convert_fusion
  63.1 34.1 %copy.40 = bf16[32,2,64,2048]{3,1,2,0:T(2,128)(2,1)} copy(bf16[32,2,64,2048]{3,0,1,2:T(8,128)(2,1)S(1)} %convolution_convert_fusion) | data formatting | bytes 33554432 | tf_op jit(solution)/shard_map/convert_element_type | solution.py:35
  97.2 85.2 %all-to-all-done.1 = bf16[32,2,64,1024]{3,2,1,0:T(8,128)(2,1)} async-done(((bf16[32,2,64,1024]{3,2,1,0:T(8,128)(2,1)}), bf16[32,2,64,1024]{3,2,1,0:T(8,128)(2,1)}, u32[]{:S(2)}, u32[]{:S(2)}) %all-to-all-start.1) | async-done | bytes 8388640 | tf_op jit(solution)/shard_map/all_to_all | solution.py:43
  182.3 5.9 %all-to-all-start = ((bf16[32,2,64,2048]{3,1,2,0:T(2,128)(2,1)}), bf16[32,2,64,2048]{3,1,2,0:T(2,128)(2,1)}, u32[]{:S(2)}, u32[]{:S(2)}) async-start(bf16[32,2,64,2048]{3,1,2,0:T(2,128)(2,1)} %copy.40), calls=%async_computation | async-start | bytes 33554432 | tf_op jit(solution)/shard_map/all_to_all | solution.py:42
  188.3 0.0 all-gather.3.cloned.1.call-start
  188.3 0.7 all-gather.3.cloned.1.call-update
  189.0 0.1 iota_compare_fusion.3
  189.1 0.0 copy-done.6
  189.1 0.1 fusion.25
  189.2 15.4 %bitcast_convert_fusion.1 = bf16[32,64,1024]{2,0,1:T(8,128)(2,1)} fusion(bf16[32,2,64,1024]{3,2,1,0:T(8,128)(2,1)} %all-to-all-done.1, pred[32,2]{0,1:T(4,128)(4,1)S(1)} %iota_compare_fusion.4, pred[32,32]{1,0:T(8,128)(4,1)S(1)} %iota_compare_fusion.3), kind=kOutput, calls=%fused_computation.5 | convolution fusion | flops 270534656 | bytes 12584000 | tf_op jit(solution)/shard_map/sm,mrd->srd/dot_general | solution.py:58
  204.6 253.4 %all-to-all-done = bf16[32,2,64,2048]{3,1,2,0:T(2,128)(2,1)} async-done(((bf16[32,2,64,2048]{3,1,2,0:T(2,128)(2,1)}), bf16[32,2,64,2048]{3,1,2,0:T(2,128)(2,1)}, u32[]{:S(2)}, u32[]{:S(2)}) %all-to-all-start) | async-done | bytes 16777248 | tf_op jit(solution)/shard_map/all_to_all | solution.py:42
  458.0 19.8 %bitcast_convert_fusion = bf16[32,64,2048]{2,0,1:T(8,128)(2,1)} fusion(bf16[32,2,64,2048]{3,1,2,0:T(2,128)(2,1)} %all-to-all-done, pred[32,2]{0,1:T(4,128)(4,1)S(1)} %iota_compare_fusion.4, pred[32,32]{1,0:T(8,128)(4,1)S(1)} %iota_compare_fusion.3), kind=kOutput, calls=%fused_computation.1 | convolution fusion | flops 541067264 | bytes 25166912 | tf_op jit(solution)/shard_map/sm,mrd->srd/dot_general | solution.py:52
  477.8 11.4 %copy.42 = bf16[32,64,2048]{2,1,0:T(8,128)(2,1)} copy(bf16[32,64,2048]{2,0,1:T(8,128)(2,1)} %bitcast_convert_fusion) | data formatting | bytes 16777216 | tf_op jit(solution)/shard_map/convert_element_type | solution.py:57
  489.2 0.0 copy-done.3
  489.2 7.1 %fusion.37 = f32[2048,512]{1,0:T(8,128)S(1)} fusion(bf16[2048,2048]{1,0:T(8,128)(2,1)} %bitcast.42, bf16[512,2048]{1,0:T(8,128)(2,1)S(1)} %copy-done.3), kind=kOutput, calls=%fused_computation.58 | convolution fusion | flops 4294967296 | bytes 14680064 | tf_op jit(solution)/shard_map/dot_general | solution.py:66
  496.3 0.7 multiply_reduce_fusion
  497.0 19.7 %all-reduce.1 = bf16[512,64]{0,1:T(8,128)(2,1)S(1)} all-reduce(f32[512,64]{0,1:T(8,128)S(1)} %multiply_reduce_fusion), channel_id=1, replica_groups=mesh['rep'=32,'mp'=4] {'mp'}, use_global_device_ids=true, to_apply=%region_2.3 | all-reduce | flops 32768 | bytes 196608 | tf_op jit(solution)/shard_map/psum | solution.py:71
  516.7 8.9 %fusion.6 = f32[512,1024,1]{1,0,2:T(8,128)} fusion(bf16[32,64,1024]{2,0,1:T(8,128)(2,1)} %bitcast_convert_fusion.1, bf16[512,64]{0,1:T(8,128)(2,1)S(1)} %all-reduce.1, bf16[512,32]{0,1:T(8,128)(2,1)S(1)} %get-tuple-element.7), kind=kOutput, calls=%fused_computation.9 | convolution fusion | flops 2148532224 | bytes 6389760 | tf_op jit(solution)/shard_map/dot_general | solution.py:75
  525.5 16.0 %fusion.10 = bf16[512,1024]{1,0:T(8,128)(2,1)} fusion(f32[512,1024,1]{1,0,2:T(8,128)} %fusion.6, bf16[512,8192]{1,0:T(8,128)(2,1)} %all-gather.3.cloned.1.call-done, bf16[8192,1024]{1,0:T(8,128)(2,1)} %param.11), kind=kOutput, calls=%fused_computation.13 | convolution fusion | flops 8590983168 | bytes 28311552 | tf_op jit(solution)/shard_map/dot_general | solution.py:19
  (17 shorter events, 0.1 us)
Async XLA Ops:
  6.5 51.7 %copy-start = (bf16[8,64,2048]{2,1,0:T(8,128)(2,1)S(1)}, bf16[8,64,2048]{2,1,0:T(8,128)(2,1)}, u32[]{:S(2)}) copy-start(bf16[8,64,2048]{2,1,0:T(8,128)(2,1)} %param.12) | copy-start | bytes 6291460
  6.5 20.9 %copy-start.2 = (s32[256]{0:T(256)S(1)}, s32[256]{0:T(256)}, u32[]{:S(2)}) copy-start(s32[256]{0:T(256)} %param.10) | copy-start | bytes 3076
  27.5 8.0 %copy-start.4 = (bf16[8,64,1024]{2,1,0:T(8,128)(2,1)S(1)}, bf16[8,64,1024]{2,1,0:T(8,128)(2,1)}, u32[]{:S(2)}) copy-start(bf16[8,64,1024]{2,1,0:T(8,128)(2,1)} %param.13) | copy-start | bytes 3145732
  51.4 130.9 %all-to-all-start.1 = ((bf16[32,2,64,1024]{3,2,1,0:T(8,128)(2,1)}), bf16[32,2,64,1024]{3,2,1,0:T(8,128)(2,1)}, u32[]{:S(2)}, u32[]{:S(2)}) async-start(bf16[32,2,64,1024]{3,2,1,0:T(8,128)(2,1)} %copy.44), calls=%async_computation.1 | async-start | bytes 16777216 | tf_op jit(solution)/shard_map/all_to_all | solution.py:43
  97.2 92.0 %copy-start.5 = (s32[1,32]{1,0:T(1,128)S(1)}, s32[1,32]{1,0:T(1,128)}, u32[]{:S(2)}) copy-start(s32[1,32]{1,0:T(1,128)} %param.9) | copy-start | bytes 388
  97.2 92.0 %copy-start.6 = (s32[512]{0:T(512)S(1)}, s32[512]{0:T(512)}, u32[]{:S(2)}) copy-start(s32[512]{0:T(512)} %param.8) | copy-start | bytes 6148
  182.3 275.7 %all-to-all-start = ((bf16[32,2,64,2048]{3,1,2,0:T(2,128)(2,1)}), bf16[32,2,64,2048]{3,1,2,0:T(2,128)(2,1)}, u32[]{:S(2)}, u32[]{:S(2)}) async-start(bf16[32,2,64,2048]{3,1,2,0:T(2,128)(2,1)} %copy.40), calls=%async_computation | async-start | bytes 33554432 | tf_op jit(solution)/shard_map/all_to_all | solution.py:42
  188.3 337.2 %all-gather.3.cloned.1.call-start = ((), (), s32[]{:S(2)}) async-start(), calls=%async_computation.2 | async-start | bytes 10485760 | tf_op jit(solution)/shard_map/all_gather | solution.py:18
  477.8 11.4 %copy-start.3 = (bf16[512,2048]{1,0:T(8,128)(2,1)S(1)}, bf16[512,2048]{1,0:T(8,128)(2,1)}, u32[]{:S(2)}) copy-start(bf16[512,2048]{1,0:T(8,128)(2,1)} %param.7) | copy-start | bytes 6291460
  525.5 16.0 %copy-start.1 = (bf16[8,64,2048]{2,1,0:T(8,128)(2,1)S(1)}, bf16[8,64,2048]{2,1,0:T(8,128)(2,1)}, u32[]{:S(2)}) copy-start(bf16[8,64,2048]{2,1,0:T(8,128)(2,1)} %param.12) | copy-start | bytes 6291460
Sparse Core Ops, SparseCore 0:
  190.8 85.4 all-gather.2
where the time goes:
time: 557 us; the launch traced here: 549 us
  waiting for transfers between devices  339 us (61%)
  matrix products  76.8 us (14%)
  local copies, waits for them, and re-layouts  63.9 us (11%)
  blocking collectives  40.5 us (7%)
  between operations  13.7 us (2%)
  starting transfers between devices  12.8 us (2%)
    all_to_all x1, waiting for transfers between devices, per_device(): lax.all_to_all(send_a, 'rep', split_axis=0, concat_axis=0, tiled=True)  253 us
    all_to_all x1, waiting for transfers between devices, per_device(): lax.all_to_all(send_b, 'rep', split_axis=0, concat_axis=0, tiled=True)  85.2 us
    convert_element_type x1, local copies, waits for them, and re-layouts, per_device(): jnp.einsum('qkj,jrd->qkrd', select, pool_a, preferred_element_type=jnp.fl...  34.1 us
    all_gather x1, blocking collectives, per_device(): all_lists = lax.all_gather(requests, 'rep', axis=0, tiled=True)  20.8 us
    dot_general x1, matrix products, per_device(): jnp.einsum('sm,mrd->srd', pick_slot, got_a.reshape(rep_count * CAP, rank_...  19.8 us
    psum x1, blocking collectives, per_device(): rank_vals = lax.psum(partial_rank, 'mp').astype(jnp.bfloat16)  19.7 us
    dot_general x1, matrix products, per_device(): base_out = jnp.dot(full_rows, q_weight, preferred_element_type=jnp.float32)  16 us
    dot_general x1, matrix products, per_device(): jnp.einsum('sm,mrd->srd', pick_slot, got_b.reshape(rep_count * CAP, rank_...  15.4 us
  transfers between devices with their start and end apart: 3, of which 2 were waited for; matrix products, arithmetic and copies ran while one was open for 19% of the time, Pallas kernels for 0%

commit v1 on v0

v1 whole, which is shorter than its diff:
```python
import jax
import jax.numpy as jnp
from jax import lax
from jax.experimental import pallas as pl
from jax.experimental.pallas import tpu as pltpu
from jax.sharding import PartitionSpec as P

MESH = pl.DeviceIdType.MESH
F32 = jnp.float32
BF16 = jnp.bfloat16

OFFS = (
    (0, 0),
    (1, 0), (3, 0), (0, 1), (0, 3),
    (1, 1), (3, 3), (1, 3), (3, 1),
    (2, 1), (1, 2), (2, 3), (3, 2),
    (2, 0), (0, 2), (2, 2),
)
CHIPS = 16
LOW_X = sum(dx << (2 * i) for i, (dx, _) in enumerate(OFFS[:8]))
HIGH_X = sum(dx << (2 * i) for i, (dx, _) in enumerate(OFFS[8:]))
LOW_Y = sum(dy << (2 * i) for i, (_, dy) in enumerate(OFFS[:8]))
HIGH_Y = sum(dy << (2 * i) for i, (_, dy) in enumerate(OFFS[8:]))
NT = (((1,), (1,)), ((), ()))
NN = (((1,), (0,)), ((), ()))


def lookup(values, i):
    found = jnp.int32(0)
    for j, value in enumerate(values):
        if value:
            found = found + value * (i == j).astype(jnp.int32)
    return found


def kernel(
    tokens, meta, table, weight, pool_a, pool_b,
    out,
    full, wts, tok, pages_a, pb_in, pb_send, pages_b, metas, smem, stage,
    part_send, part_recv, zsum, zrecv, ranks, delta_send, delta_recv, acc,
    z_s, z_r, tok_s, tok_r, a_s, a_r, ac_s, ac_r, b_s, b_r, bc_s, bc_r, m_s, m_r,
    p_s, p_r, zp_s, zp_r, zq_s, zq_r, k_s, k_r, d_s, d_r, loc,
):
    rep = lax.axis_index("rep")
    z = lax.axis_index("mp")
    x, y, core = rep // 8, (rep // 2) % 4, rep % 2
    chip = x * 4 + y

    def ahead(i):
        dx, dy = OFFS[i]
        return (((x + dx) % 4) * 4 + (y + dy) % 4) * 2 + core

    def behind(i):
        dx, dy = OFFS[i]
        return (((x + 4 - dx) % 4) * 4 + (y + 4 - dy) % 4) * 2 + core

    def behind_loop(i):
        dx = lookup([o[0] for o in OFFS], i)
        dy = lookup([o[1] for o in OFFS], i)
        return (((x + 4 - dx) % 4) * 4 + (y + 4 - dy) % 4) * 2 + core

    def zat(d):
        return (z + d) % 4

    sibling = rep + 1 - 2 * core

    def remote(src, dst, ss, rs, dev):
        return pltpu.make_async_remote_copy(
            src_ref=src, dst_ref=dst, send_sem=ss, recv_sem=rs, device_id=dev, device_id_type=MESH
        )

    local = [
        pltpu.make_async_copy(tokens, full.at[z], loc.at[0]),
        pltpu.make_async_copy(pool_b, pb_in, loc.at[1]),
        pltpu.make_async_copy(tokens.at[:, pl.ds(chip * 128, 128)], tok.at[0], loc.at[2]),
        pltpu.make_async_copy(
            pool_a.at[:, :, pl.ds(chip * 128, 128)], pages_a.at[pl.ds(rep * 8, 8)], loc.at[3]
        ),
    ]
    wloads = [
        pltpu.make_async_copy(weight.at[pl.ds(zat(d) * 2048, 2048)], wts.at[d], loc.at[4 + d])
        for d in range(4)
    ]

    barrier = pltpu.get_barrier_semaphore()
    for i in range(1, CHIPS):
        pl.semaphore_signal(barrier, inc=1, device_id=(ahead(i), z), device_id_type=MESH)
    pl.semaphore_signal(barrier, inc=1, device_id=(sibling, z), device_id_type=MESH)
    for d in range(1, 4):
        pl.semaphore_signal(barrier, inc=1, device_id=(rep, zat(d)), device_id_type=MESH)
    for copy in (local[1], local[0], local[2], local[3], wloads[0], wloads[3], wloads[1], wloads[2]):
        copy.start()
    metas[0] = meta[...]
    pl.semaphore_wait(barrier, CHIPS - 1 + 4)

    def rows(c):
        return pl.ds(c * 128, 128)

    def z_own(way, c):
        dev = (rep, zat(1 if way == 0 else 3))
        return remote(tokens.at[rows(c)], full.at[z, rows(c)], z_s.at[way, c], z_r.at[way, c], dev)

    def z_relay(way, n):
        c = n + 2 * way
        src = zat(3 if way == 0 else 1)
        dev = (rep, zat(1 if way == 0 else 3))
        part = full.at[src, rows(c)]
        return remote(part, part, z_s.at[way, 4 + n], z_r.at[way, 4 + n], dev)

    for n in range(4):
        z_own(0, n).start()
        z_own(1, (n + 2) % 4).start()

    def send_meta(i):
        return remote(meta, metas.at[i], m_s.at[i], m_r.at[i], (ahead(i), z))

    def send_a(i):
        to = ahead(i)
        return remote(
            pool_a.at[:, :, pl.ds((to // 2) * 128, 128)], pages_a.at[pl.ds(rep * 8, 8)],
            a_s.at[i], a_r.at[i], (to, z),
        )

    def send_tok(i):
        to = ahead(i)
        return remote(
            tokens.at[:, pl.ds((to // 2) * 128, 128)], tok.at[i], tok_s.at[i], tok_r.at[i], (to, z)
        )

    def send_b(i):
        to = ahead(i)
        return remote(
            pb_send.at[to // 2], pages_b.at[pl.ds(rep * 4, 4)], b_s.at[i], b_r.at[i], (to, z)
        )

    for i in range(1, CHIPS):
        send_a(i).start()
    for i in range(1, CHIPS):
        send_meta(i).start()
    for i in range(1, CHIPS):
        send_tok(i).start()

    local[1].wait()

    @pl.loop(0, 4)
    def _(q):
        for j in range(8):
            block = pb_in[q, :, j * 128 : (j + 1) * 128].astype(F32).T.astype(BF16)
            pb_send[2 * j, q] = block[:64]
            pb_send[2 * j + 1, q] = block[64:]

    pages_b[pl.ds(rep * 4, 4)] = pb_send[chip]
    for i in range(1, CHIPS):
        send_b(i).start()

    def base_block(d, first):
        m = zat(d)

        @pl.loop(0, 4)
        def _(n):
            cols = pl.ds(pl.multiple_of(n * 256, 256), 256)
            term = jnp.dot(full[m], wts[d, :, cols], preferred_element_type=F32)
            if first:
                acc[:, cols] = term
            else:
                acc[:, cols] += term

    local[0].wait()
    wloads[0].wait()
    base_block(0, True)

    def relay_a(i):
        owner = behind(i)
        piece = pages_a.at[pl.ds(owner * 8, 8)]
        return remote(piece, piece, ac_s.at[i], ac_r.at[i], (sibling, z))

    def relay_b(i):
        owner = behind(i)
        piece = pages_b.at[pl.ds(owner * 4, 4)]
        return remote(piece, piece, bc_s.at[i], bc_r.at[i], (sibling, z))

    local[3].wait()
    relay_a(0).start()
    relay_b(0).start()
    for i in range(1, CHIPS):
        send_a(i).wait_recv()
        relay_a(i).start()
        if i == 8:
            for n in range(2):
                z_own(0, n).wait_recv()
                z_relay(0, n).start()
                z_own(1, n + 2).wait_recv()
                z_relay(1, n).start()
    for i in range(1, CHIPS):
        send_meta(i).wait_recv()
    smem_copy = pltpu.make_async_copy(metas, smem, loc.at[8])
    smem_copy.start()
    for i in range(CHIPS):
        relay_a(i).wait_recv()
    smem_copy.wait()

    def half_ids(i, h):
        own = metas[i]
        return jnp.concatenate([own[4 + 2 * h : 5 + 2 * h], own[5 + 2 * h : 6 + 2 * h]], axis=1)

    def shrink(i):
        for s in range(32):
            stage[s * 64 : (s + 1) * 64] = pages_a[table[smem[i, 0, s]]]
        for h in range(2):
            ids = half_ids(i, h)
            feats = tok[i, h * 256 : (h + 1) * 256]
            total = jnp.zeros((64, 256), F32)
            for g in range(4):
                got = lax.dot_general(
                    stage[g * 512 : (g + 1) * 512], feats, NT, preferred_element_type=F32
                )
                for s in range(8):
                    hit = ids == smem[i, 0, g * 8 + s]
                    total = jnp.where(hit, got[s * 64 : (s + 1) * 64], total)
            part_send[i, :, h * 256 : (h + 1) * 256] = total

    def send_part(i, dev):
        return remote(part_send.at[i], part_recv.at[i], p_s.at[i], p_r.at[i], (dev, z))

    local[2].wait()

    @pl.loop(0, CHIPS)
    def _(i):
        @pl.when(i > 0)
        def _():
            remote(tok.at[i], tok.at[i], tok_s.at[i], tok_r.at[i], (rep, zat(1))).wait_recv()

        shrink(i)

        @pl.when(i > 0)
        def _():
            send_part(i, behind_loop(i)).start()

    for n in range(4):
        if n >= 2:
            z_own(0, n).wait_recv()
            z_own(1, (n + 2) % 4).wait_recv()
    wloads[3].wait()
    base_block(3, False)
    wloads[1].wait()
    base_block(1, False)

    for i in range(1, CHIPS):
        send_b(i).wait_recv()
        relay_b(i).start()

    for i in range(1, CHIPS):
        send_part(i, rep).wait_recv()
    for q in range(4):
        cols = slice(q * 128, (q + 1) * 128)
        total = part_send[0, :, cols]
        for i in range(1, CHIPS):
            total = total + part_recv[i, :, cols]
        zsum[q] = total

    def send_zsum(d):
        to = zat(d)
        return remote(zsum.at[to], zrecv.at[d], zp_s.at[d], zp_r.at[d], (rep, to))

    for d in (2, 1, 3):
        send_zsum(d).start()
    for d in range(1, 4):
        send_zsum(d).wait_recv()
    ranks[0, z] = (zsum[z] + zrecv[1] + zrecv[2] + zrecv[3]).astype(BF16)

    def send_quarter(d):
        part = ranks.at[0, z]
        return remote(part, part, zq_s.at[d], zq_r.at[d], (rep, zat(d)))

    for d in (2, 1, 3):
        send_quarter(d).start()
    for d in range(1, 4):
        send_quarter(d).wait_recv()

    def send_rank(i):
        return remote(ranks.at[0], ranks.at[i], k_s.at[i], k_r.at[i], (ahead(i), z))

    for i in range(1, CHIPS):
        send_rank(i).start()
    for i in range(CHIPS):
        relay_b(i).wait_recv()

    def expand(i):
        for s in range(32):
            stage[s * 64 : (s + 1) * 64] = pages_b[table[smem[i, 0, s]] // 2]
        for h in range(2):
            ids = half_ids(i, h)
            odd = jnp.zeros((1, 256), jnp.int32)
            for s in range(32):
                name = smem[i, 0, s]
                odd = jnp.where(ids == name, table[name] % 2, odd)
            vals = jnp.concatenate([ranks[i, 2 * h], ranks[i, 2 * h + 1]], axis=1).astype(F32)
            vals = jnp.concatenate(
                [jnp.where(odd == 0, vals, 0.0), jnp.where(odd == 1, vals, 0.0)], axis=0
            ).astype(BF16)
            total = jnp.zeros((64, 256), F32)
            for g in range(4):
                got = lax.dot_general(
                    stage[g * 512 : (g + 1) * 512], vals, NN, preferred_element_type=F32
                )
                for s in range(8):
                    hit = ids == smem[i, 0, g * 8 + s]
                    total = jnp.where(hit, got[s * 64 : (s + 1) * 64], total)
            delta_send[i, :, h * 256 : (h + 1) * 256] = total.astype(BF16)

    def send_delta(i, dev):
        return remote(delta_send.at[i], delta_recv.at[chip], d_s.at[i], d_r.at[i], (dev, z))

    @pl.loop(0, CHIPS)
    def _(i):
        @pl.when(i > 0)
        def _():
            remote(ranks.at[i], ranks.at[i], k_s.at[i], k_r.at[i], (rep, zat(1))).wait_recv()

        expand(i)

        @pl.when(i > 0)
        def _():
            send_delta(i, behind_loop(i)).start()

    delta_recv[chip] = delta_send[0]

    for n in range(2):
        z_relay(0, n).wait_recv()
        z_relay(1, n).wait_recv()
    wloads[2].wait()
    base_block(2, False)

    for i in range(1, CHIPS):
        send_delta(i, rep).wait_recv()

    @pl.loop(0, 8)
    def _(j):
        cols = pl.ds(pl.multiple_of(j * 128, 128), 128)
        block = jnp.concatenate([delta_recv[2 * j], delta_recv[2 * j + 1]], axis=0)
        out[:, cols] = (acc[:, cols] + block.astype(F32).T).astype(BF16)

    for way in range(2):
        for n in range(4):
            z_own(way, n).wait_send()
        for n in range(2):
            z_relay(way, n).wait_send()
    for i in range(1, CHIPS):
        send_a(i).wait_send()
        send_meta(i).wait_send()
        send_tok(i).wait_send()
        send_b(i).wait_send()
        send_part(i, rep).wait_send()
        send_rank(i).wait_send()
        send_delta(i, rep).wait_send()
    for i in range(CHIPS):
        relay_a(i).wait_send()
        relay_b(i).wait_send()
    for d in range(1, 4):
        send_zsum(d).wait_send()
        send_quarter(d).wait_send()


def per_device(tokens, tok_adapter, requests, owner_table, q_weight, pool_a, pool_b):
    lists = jnp.pad(requests, ((0, 3), (0, 96)))
    meta = jnp.concatenate([lists, tok_adapter.reshape(4, 128)], axis=0)
    dma = pltpu.SemaphoreType.DMA
    anywhere = pl.BlockSpec(memory_space=pl.ANY)
    vmem = pl.BlockSpec(memory_space=pltpu.VMEM)
    smem = pl.BlockSpec(memory_space=pltpu.SMEM)
    return pl.pallas_call(
        kernel,
        out_shape=jax.ShapeDtypeStruct((512, 1024), BF16),
        in_specs=[anywhere, vmem, smem, anywhere, anywhere, anywhere],
        out_specs=vmem,
        scratch_shapes=[
            pltpu.VMEM((4, 512, 2048), BF16),
            pltpu.VMEM((4, 2048, 1024), BF16),
            pltpu.VMEM((16, 512, 128), BF16),
            pltpu.VMEM((256, 64, 128), BF16),
            pltpu.VMEM((4, 128, 1024), BF16),
            pltpu.VMEM((16, 4, 64, 128), BF16),
            pltpu.VMEM((128, 64, 128), BF16),
            pltpu.VMEM((16, 8, 128), jnp.int32),
            pltpu.SMEM((16, 8, 128), jnp.int32),
            pltpu.VMEM((2048, 128), BF16),
            pltpu.VMEM((16, 64, 512), F32),
            pltpu.VMEM((16, 64, 512), F32),
            pltpu.VMEM((4, 64, 128), F32),
            pltpu.VMEM((4, 64, 128), F32),
            pltpu.VMEM((16, 4, 64, 128), BF16),
            pltpu.VMEM((16, 64, 512), BF16),
            pltpu.VMEM((16, 64, 512), BF16),
            pltpu.VMEM((512, 1024), F32),
            dma((2, 6)), dma((2, 6)),
            dma((16,)), dma((16,)),
            dma((16,)), dma((16,)),
            dma((16,)), dma((16,)),
            dma((16,)), dma((16,)),
            dma((16,)), dma((16,)),
            dma((16,)), dma((16,)),
            dma((16,)), dma((16,)),
            dma((4,)), dma((4,)),
            dma((4,)), dma((4,)),
            dma((16,)), dma((16,)),
            dma((16,)), dma((16,)),
            dma((9,)),
        ],
        compiler_params=pltpu.CompilerParams(
            collective_id=1, has_side_effects=True, vmem_limit_bytes=62 * 2**20
        ),
        cost_estimate=pl.CostEstimate(
            flops=20_000_000_000, bytes_accessed=30_000_000, transcendentals=0
        ),
        name="lora_projection",
    )(tokens, meta, owner_table, q_weight, pool_a, pool_b.reshape(4, 128, 1024))


def solution(mesh):
    in_specs = (
        P("rep", "mp"),
        P("rep"),
        P("rep", None),
        P(),
        P(None, "mp"),
        P("rep", None, "mp"),
        P("rep", None, "mp"),
    )
    out_specs = P("rep", "mp")
    return jax.shard_map(
        per_device, mesh=mesh, in_specs=in_specs, out_specs=out_specs, check_vma=False
    )
```

time: 557 us -> 138 us (0.25)
  the two profiles are of different devices: /device:TPU:12 before, /device:TPU:0 now
where the time goes in v1:
time: 138 us; the launch traced here: 137 us
  Pallas kernels  134 us (97%)
  local copies, waits for them, and re-layouts  2.26 us (2%)
    pallas_call x1, Pallas kernels, per_device(): pl.pallas_call(kernel, out_shape=jax.ShapeDtypeStruct((512, 1024), BF16),...  134 us

profile of v1, /device:TPU:0, one launch (start us, length us, event | category | flops | bytes accessed | tf_op | source)
XLA Modules:
  0.0 137.2 jit_solution(6295085079053722257)
XLA Ops:
  0.0 1.3 pad_add_fusion.meta
  1.3 133.7 %lora_projection.1 = bf16[512,1024]{1,0:T(8,128)(2,1)} custom-call(bf16[512,2048]{1,0:T(8,128)(2,1)} %tokens.1, s32[8,128]{1,0:T(8,128)} %pad_add_fusion.meta, s32[256]{0:T(256)} %table.1, bf16[8192,1024]{1,0:T(8,128)(2,1)} %weight.1, bf16[8,64,2048]{2,1,0:T(8,128)(2,1)} %pool_a.1, bf16[4,128,1024]{2,1,0:T(8,128)(2,1)} %bitcast.3), custom_call_target="tpu_custom_call" | custom-call | flops 20000000000 | bytes 30000000 | tf_op jit(solution)/shard_map/lora_projection/pallas_call | solution.py:371
  135.0 2.3 %copy.9 = bf16[512,1024]{1,0:T(8,128)(2,1)} copy(bf16[512,1024]{1,0:T(8,128)(2,1)} %lora_projection.1) | data formatting | bytes 2097152

commit v2 on v1

v2 whole, which is shorter than its diff:
```python
import jax
import jax.numpy as jnp
from jax import lax
from jax.experimental import pallas as pl
from jax.experimental.pallas import tpu as pltpu
from jax.sharding import PartitionSpec as P

MESH = pl.DeviceIdType.MESH
F32 = jnp.float32
BF16 = jnp.bfloat16

OFFS = (
    (0, 0),
    (1, 0), (3, 0), (0, 1), (0, 3),
    (1, 1), (3, 3), (1, 3), (3, 1),
    (2, 1), (1, 2), (2, 3), (3, 2),
    (2, 0), (0, 2), (2, 2),
)
CHIPS = 16
NT = (((1,), (1,)), ((), ()))
NN = (((1,), (0,)), ((), ()))


def lookup(values, i):
    found = jnp.int32(0)
    for j, value in enumerate(values):
        if value:
            found = found + value * (i == j).astype(jnp.int32)
    return found


def kernel(
    tokens, meta, table, weight, pool_a, pool_b,
    out,
    full, wts, own_tok, tok, pages_a, pb_in, pb_send, pages_b, metas, smem, pair, odds, stage,
    part_send, part_recv, mid, end, zsum, zrecv, ranks, delta_send, delta_recv, acc,
    z_s, z_r, tok_s, tok_r, a_s, a_r, ac_s, ac_r, b_s, b_r, bc_s, bc_r, m_s, m_r,
    px_s, px_r, py_s, py_r, ex_s, ex_r, ey_s, ey_r, zp_s, zp_r, zq_s, zq_r, k_s, k_r, d_s, d_r, loc,
):
    rep = lax.axis_index("rep")
    z = lax.axis_index("mp")
    x, y, core = rep // 8, (rep // 2) % 4, rep % 2
    chip = x * 4 + y

    def rep_at(cx, cy):
        return (cx * 4 + cy) * 2 + core

    def ahead(i):
        dx, dy = OFFS[i]
        return (((x + dx) % 4) * 4 + (y + dy) % 4) * 2 + core

    def behind(i):
        dx, dy = OFFS[i]
        return (((x + 4 - dx) % 4) * 4 + (y + 4 - dy) % 4) * 2 + core

    def ahead_loop(i):
        dx = lookup([o[0] for o in OFFS], i)
        dy = lookup([o[1] for o in OFFS], i)
        return (((x + dx) % 4) * 4 + (y + dy) % 4) * 2 + core

    def behind_loop(i):
        dx = lookup([o[0] for o in OFFS], i)
        dy = lookup([o[1] for o in OFFS], i)
        return (((x + 4 - dx) % 4) * 4 + (y + 4 - dy) % 4) * 2 + core

    def zat(d):
        return (z + d) % 4

    sibling = rep + 1 - 2 * core

    def remote(src, dst, ss, rs, dev):
        return pltpu.make_async_remote_copy(
            src_ref=src, dst_ref=dst, send_sem=ss, recv_sem=rs, device_id=dev, device_id_type=MESH
        )

    local = [
        pltpu.make_async_copy(tokens, full.at[z], loc.at[0]),
        pltpu.make_async_copy(pool_b, pb_in, loc.at[1]),
        pltpu.make_async_copy(tokens.at[:, pl.ds(chip * 128, 128)], own_tok, loc.at[2]),
        pltpu.make_async_copy(
            pool_a.at[:, :, pl.ds(chip * 128, 128)], pages_a.at[pl.ds(rep * 8, 8)], loc.at[3]
        ),
    ]
    wloads = [
        pltpu.make_async_copy(weight.at[pl.ds(zat(d) * 2048, 2048)], wts.at[d], loc.at[4 + d])
        for d in range(4)
    ]

    barrier = pltpu.get_barrier_semaphore()
    for i in range(1, CHIPS):
        pl.semaphore_signal(barrier, inc=1, device_id=(ahead(i), z), device_id_type=MESH)
    pl.semaphore_signal(barrier, inc=1, device_id=(sibling, z), device_id_type=MESH)
    for d in range(1, 4):
        pl.semaphore_signal(barrier, inc=1, device_id=(rep, zat(d)), device_id_type=MESH)
    for copy in (local[1], local[0], local[2], local[3], wloads[0], wloads[3], wloads[1], wloads[2]):
        copy.start()
    metas[0] = meta[...]
    pl.semaphore_wait(barrier, CHIPS - 1 + 4)

    def rows(c):
        return pl.ds(c * 128, 128)

    def z_own(way, c):
        dev = (rep, zat(1 if way == 0 else 3))
        return remote(tokens.at[rows(c)], full.at[z, rows(c)], z_s.at[way, c], z_r.at[way, c], dev)

    def z_relay(way, n):
        c = n + 2 * way
        src = zat(3 if way == 0 else 1)
        dev = (rep, zat(1 if way == 0 else 3))
        part = full.at[src, rows(c)]
        return remote(part, part, z_s.at[way, 4 + n], z_r.at[way, 4 + n], dev)

    def send_meta(i):
        return remote(meta, metas.at[i], m_s.at[i], m_r.at[i], (ahead(i), z))

    def send_a(i):
        to = ahead(i)
        return remote(
            pool_a.at[:, :, pl.ds((to // 2) * 128, 128)], pages_a.at[pl.ds(rep * 8, 8)],
            a_s.at[i], a_r.at[i], (to, z),
        )

    def send_tok(half, i, to):
        n = half * CHIPS + i
        start = pl.multiple_of((to // 2) * 128, 128)
        return remote(
            tokens.at[pl.ds(half * 256, 256), pl.ds(start, 128)], tok.at[half, i],
            tok_s.at[n], tok_r.at[n], (to, z),
        )

    def send_b(i):
        to = ahead(i)
        return remote(
            pb_send.at[to // 2], pages_b.at[pl.ds(rep * 4, 4)], b_s.at[i], b_r.at[i], (to, z)
        )

    def relay_a(i):
        piece = pages_a.at[pl.ds(behind(i) * 8, 8)]
        return remote(piece, piece, ac_s.at[i], ac_r.at[i], (sibling, z))

    def relay_b(i):
        piece = pages_b.at[pl.ds(behind(i) * 4, 4)]
        return remote(piece, piece, bc_s.at[i], bc_r.at[i], (sibling, z))

    for i in range(1, CHIPS):
        send_a(i).start()
    for n in range(2):
        z_own(0, n).start()
        z_own(1, n + 2).start()
    for i in range(1, CHIPS):
        send_meta(i).start()
    for i in range(1, CHIPS):
        send_tok(0, i, ahead(i)).start()

    local[1].wait()

    @pl.loop(0, 4)
    def _(q):
        for j in range(8):
            block = pb_in[q, :, j * 128 : (j + 1) * 128].astype(F32).T.astype(BF16)
            pb_send[2 * j, q] = block[:64]
            pb_send[2 * j + 1, q] = block[64:]

    pages_b[pl.ds(rep * 4, 4)] = pb_send[chip]

    def base_block(d, first):
        m = zat(d)

        @pl.loop(0, 4)
        def _(n):
            cols = pl.ds(pl.multiple_of(n * 256, 256), 256)
            term = jnp.dot(full[m], wts[d, :, cols], preferred_element_type=F32)
            if first:
                acc[:, cols] = term
            else:
                acc[:, cols] += term

    local[3].wait()
    relay_a(0).start()
    relay_b(0).start()
    local[0].wait()
    wloads[0].wait()
    base_block(0, True)

    for i in range(1, CHIPS):
        send_a(i).wait_recv()
        relay_a(i).start()
        send_tok(1, i, ahead(i)).start()
    for n in range(2):
        z_own(0, n + 2).start()
        z_own(1, n).start()
    for i in range(1, CHIPS):
        send_meta(i).wait_recv()
    smem_copy = pltpu.make_async_copy(metas, smem, loc.at[8])
    smem_copy.start()
    for i in range(CHIPS):
        relay_a(i).wait_recv()
    smem_copy.wait()
    local[2].wait()
    tok[0, 0] = own_tok[:256]
    tok[1, 0] = own_tok[256:]

    def ids_of(i, half):
        own = metas[i]
        first = 4 + 2 * half
        return jnp.concatenate([own[first : first + 1], own[first + 1 : first + 2]], axis=1)

    def by_slot(i, ids, left, right, dims):
        total = jnp.zeros((64, 256), F32)
        for g in range(4):
            got = lax.dot_general(
                left[g * 512 : (g + 1) * 512], right, dims, preferred_element_type=F32
            )
            for s in range(8):
                hit = ids == smem[i, 0, g * 8 + s]
                total = jnp.where(hit, got[s * 64 : (s + 1) * 64], total)
        return total

    def send_px(half, i, dev):
        n = half * CHIPS + i
        rows = pl.ds(0, 32)
        return remote(
            part_send.at[half, i, rows], part_recv.at[half, i, rows], px_s.at[n], px_r.at[n],
            (dev, z),
        )

    def send_py(half, i, dev):
        n = half * CHIPS + i
        rows = pl.ds(32, 32)
        return remote(
            part_send.at[half, i, rows], part_recv.at[half, i, rows], py_s.at[n], py_r.at[n],
            (dev, z),
        )

    def shrink(half):
        @pl.loop(0, CHIPS)
        def _(i):
            @pl.when(i > 0)
            def _():
                send_tok(half, i, rep).wait_recv()

            for s in range(32):
                stage[s * 64 : (s + 1) * 64] = pages_a[table[smem[i, 0, s]]]
            part_send[half, i] = by_slot(i, ids_of(i, half), stage, tok[half, i], NT)

            dx = lookup([o[0] for o in OFFS], i)
            dy = lookup([o[1] for o in OFFS], i)

            @pl.when(dx > 0)
            def _():
                send_px(half, i, rep_at((x + 4 - dx) % 4, y)).start()

            @pl.when(dy > 0)
            def _():
                send_py(half, i, rep_at(x, (y + 4 - dy) % 4)).start()

    shrink(0)
    for n in range(2):
        z_own(0, n).wait_recv()
        z_relay(0, n).start()
        z_own(1, n + 2).wait_recv()
        z_relay(1, n).start()
    shrink(1)

    def send_ex(half, dy):
        n = half * 4 + dy
        dev = rep_at(x, (y + 4 - dy) % 4)
        return remote(mid.at[half, 0, dy], end.at[half, 0, dy], ex_s.at[n], ex_r.at[n], (dev, z))

    def send_ey(half, dx):
        n = half * 4 + dx
        dev = rep_at((x + 4 - dx) % 4, y)
        return remote(mid.at[half, 1, dx], end.at[half, 1, dx], ey_s.at[n], ey_r.at[n], (dev, z))

    def first_sums(half):
        for o in (1, 3, 2, 0):
            for d in range(1, 4):
                send_px(half, OFFS.index((d, o)), rep).wait_recv()
            total = part_send[half, OFFS.index((0, o)), :32]
            for d in range(1, 4):
                total = total + part_recv[half, OFFS.index((d, o)), :32]
            mid[half, 0, o] = total
            if o:
                send_ex(half, o).start()
            for d in range(1, 4):
                send_py(half, OFFS.index((o, d)), rep).wait_recv()
            total = part_send[half, OFFS.index((o, 0)), 32:]
            for d in range(1, 4):
                total = total + part_recv[half, OFFS.index((o, d)), 32:]
            mid[half, 1, o] = total
            if o:
                send_ey(half, o).start()

    def collect(half):
        for axis in range(2):
            total = mid[half, axis, 0]
            for o in (1, 3, 2):
                (send_ey if axis else send_ex)(half, o).wait_recv()
                total = total + end[half, axis, o]
            zsum[half, 2 * axis] = total[:16]
            zsum[half, 2 * axis + 1] = total[16:]

    def send_zsum(half, d):
        to = zat(d)
        n = half * 4 + d
        return remote(zsum.at[half, to], zrecv.at[half, d], zp_s.at[n], zp_r.at[n], (rep, to))

    def start_sums(half):
        for d in (2, 1, 3):
            send_zsum(half, d).start()

    def send_rank(half, i, to):
        n = half * CHIPS + i
        return remote(ranks.at[half, z, 0], ranks.at[half, z, i], k_s.at[n], k_r.at[n], (to, z))

    def pass_rank(half, g, d):
        n = (half * 4 + g) * 4 + d
        part = ranks.at[half, z, pl.ds(g * 4, 4)]
        return remote(part, part, zq_s.at[n], zq_r.at[n], (rep, zat(d)))

    def start_ranks(half):
        for d in range(1, 4):
            send_zsum(half, d).wait_recv()
        ranks[half, z, 0] = (
            zsum[half, z] + zrecv[half, 1] + zrecv[half, 2] + zrecv[half, 3]
        ).astype(BF16)
        for i in range(1, CHIPS):
            send_rank(half, i, ahead(i)).start()

    def pass_ranks(half):
        for g in range(4):
            for i in range(max(1, 4 * g), 4 * g + 4):
                send_rank(half, i, rep).wait_recv()
            for d in (2, 1, 3):
                pass_rank(half, g, d).start()

    @pl.loop(0, CHIPS)
    def _(i):
        ids = jnp.concatenate([ids_of(i, 0), ids_of(i, 1)], axis=1)
        odd = jnp.zeros((1, 512), jnp.int32)
        for s in range(32):
            name = smem[i, 0, s]
            page = table[name]
            pair[i, s] = page >> 1
            odd = jnp.where(ids == name, page & 1, odd)
        odds[i] = odd

    first_sums(0)
    collect(0)
    start_sums(0)
    first_sums(1)
    for i in range(1, CHIPS):
        send_b(i).start()
    start_ranks(0)
    collect(1)
    start_sums(1)
    for n in range(2):
        z_own(0, n + 2).wait_recv()
    wloads[3].wait()
    base_block(3, False)
    start_ranks(1)
    pass_ranks(0)
    pass_ranks(1)
    for n in range(2):
        z_own(1, n).wait_recv()
    wloads[1].wait()
    for i in range(1, CHIPS):
        send_b(i).wait_recv()
        relay_b(i).start()
    base_block(1, False)
    for i in range(CHIPS):
        relay_b(i).wait_recv()

    def send_delta(i, dev):
        return remote(delta_send.at[i], delta_recv.at[chip], d_s.at[i], d_r.at[i], (dev, z))

    @pl.loop(0, CHIPS)
    def _(i):
        for s in range(32):
            stage[s * 64 : (s + 1) * 64] = pages_b[pair[i, s]]

        @pl.when(i % 4 == 0)
        def _():
            for half in range(2):
                for d in range(1, 4):
                    pass_rank(half, i // 4, d).wait_recv()

        for half in range(2):
            odd = odds[i, :, half * 256 : (half + 1) * 256]
            vals = jnp.concatenate([ranks[half, q, i] for q in range(4)], axis=0).astype(F32)
            vals = jnp.concatenate(
                [jnp.where(odd == 0, vals, 0.0), jnp.where(odd == 1, vals, 0.0)], axis=0
            ).astype(BF16)
            delta_send[i, half] = by_slot(i, ids_of(i, half), stage, vals, NN).astype(BF16)

        @pl.when(i > 0)
        def _():
            send_delta(i, behind_loop(i)).start()

    delta_recv[chip] = delta_send[0]

    for n in range(2):
        z_relay(0, n).wait_recv()
        z_relay(1, n).wait_recv()
    wloads[2].wait()
    base_block(2, False)

    for i in range(1, CHIPS):
        send_delta(i, rep).wait_recv()
    for half in range(2):

        @pl.loop(0, 8)
        def _(j):
            part = pl.ds(half * 256, 256)
            cols = pl.ds(pl.multiple_of(j * 128, 128), 128)
            block = jnp.concatenate(
                [delta_recv[2 * j, half], delta_recv[2 * j + 1, half]], axis=0
            )
            out[part, cols] = (acc[part, cols] + block.astype(F32).T).astype(BF16)

    for way in range(2):
        for n in range(4):
            z_own(way, n).wait_send()
        for n in range(2):
            z_relay(way, n).wait_send()
    for i in range(1, CHIPS):
        send_a(i).wait_send()
        send_meta(i).wait_send()
        send_b(i).wait_send()
        send_delta(i, rep).wait_send()
        for half in range(2):
            send_tok(half, i, rep).wait_send()
            send_rank(half, i, rep).wait_send()
    for i in range(CHIPS):
        relay_a(i).wait_send()
        relay_b(i).wait_send()
    for half in range(2):
        for i, (dx, dy) in enumerate(OFFS):
            if dx:
                send_px(half, i, rep).wait_send()
            if dy:
                send_py(half, i, rep).wait_send()
        for d in range(1, 4):
            send_ex(half, d).wait_send()
            send_ey(half, d).wait_send()
            send_zsum(half, d).wait_send()
            for g in range(4):
                pass_rank(half, g, d).wait_send()


def per_device(tokens, tok_adapter, requests, owner_table, q_weight, pool_a, pool_b):
    lists = jnp.pad(requests, ((0, 3), (0, 96)))
    meta = jnp.concatenate([lists, tok_adapter.reshape(4, 128)], axis=0)
    dma = pltpu.SemaphoreType.DMA
    anywhere = pl.BlockSpec(memory_space=pl.ANY)
    vmem = pl.BlockSpec(memory_space=pltpu.VMEM)
    smem = pl.BlockSpec(memory_space=pltpu.SMEM)
    return pl.pallas_call(
        kernel,
        out_shape=jax.ShapeDtypeStruct((512, 1024), BF16),
        in_specs=[anywhere, vmem, smem, anywhere, anywhere, anywhere],
        out_specs=vmem,
        scratch_shapes=[
            pltpu.VMEM((4, 512, 2048), BF16),
            pltpu.VMEM((4, 2048, 1024), BF16),
            pltpu.VMEM((512, 128), BF16),
            pltpu.VMEM((2, 16, 256, 128), BF16),
            pltpu.VMEM((256, 64, 128), BF16),
            pltpu.VMEM((4, 128, 1024), BF16),
            pltpu.VMEM((16, 4, 64, 128), BF16),
            pltpu.VMEM((128, 64, 128), BF16),
            pltpu.VMEM((16, 8, 128), jnp.int32),
            pltpu.SMEM((16, 8, 128), jnp.int32),
            pltpu.SMEM((16, 32), jnp.int32),
            pltpu.VMEM((16, 1, 512), jnp.int32),
            pltpu.VMEM((2048, 128), BF16),
            pltpu.VMEM((2, 16, 64, 256), F32),
            pltpu.VMEM((2, 16, 64, 256), F32),
            pltpu.VMEM((2, 2, 4, 32, 256), F32),
            pltpu.VMEM((2, 2, 4, 32, 256), F32),
            pltpu.VMEM((2, 4, 16, 256), F32),
            pltpu.VMEM((2, 4, 16, 256), F32),
            pltpu.VMEM((2, 4, 16, 16, 256), BF16),
            pltpu.VMEM((16, 2, 64, 256), BF16),
            pltpu.VMEM((16, 2, 64, 256), BF16),
            pltpu.VMEM((512, 1024), F32),
            dma((2, 6)), dma((2, 6)),
            dma((32,)), dma((32,)),
            dma((16,)), dma((16,)),
            dma((16,)), dma((16,)),
            dma((16,)), dma((16,)),
            dma((16,)), dma((16,)),
            dma((16,)), dma((16,)),
            dma((32,)), dma((32,)),
            dma((32,)), dma((32,)),
            dma((8,)), dma((8,)),
            dma((8,)), dma((8,)),
            dma((8,)), dma((8,)),
            dma((32,)), dma((32,)),
            dma((32,)), dma((32,)),
            dma((16,)), dma((16,)),
            dma((9,)),
        ],
        compiler_params=pltpu.CompilerParams(
            collective_id=1, has_side_effects=True, vmem_limit_bytes=62 * 2**20
        ),
        cost_estimate=pl.CostEstimate(
            flops=20_000_000_000, bytes_accessed=30_000_000, transcendentals=0
        ),
        name="lora_projection",
    )(tokens, meta, owner_table, q_weight, pool_a, pool_b.reshape(4, 128, 1024))


def solution(mesh):
    in_specs = (
        P("rep", "mp"),
        P("rep"),
        P("rep", None),
        P(),
        P(None, "mp"),
        P("rep", None, "mp"),
        P("rep", None, "mp"),
    )
    out_specs = P("rep", "mp")
    return jax.shard_map(
        per_device, mesh=mesh, in_specs=in_specs, out_specs=out_specs, check_vma=False
    )
```

time: 138 us -> 125 us (0.906)
  Pallas kernels: 134 us -> 122 us
    pallas_call x1, Pallas kernels: 134 us -> 122 us  [per_device(): pl.pallas_call(kernel, out_shape=jax.ShapeDtypeStruct((512, 1024), BF16),...]
where the time goes in v2:
time: 125 us
  Pallas kernels  122 us (98%)
  local copies, waits for them, and re-layouts  2.26 us (2%)
  other arithmetic  1.3 us (1%)
    pallas_call x1, Pallas kernels, per_device(): pl.pallas_call(kernel, out_shape=jax.ShapeDtypeStruct((512, 1024), BF16),...  122 us

profile of v2, /device:TPU:0, one launch (start us, length us, event | category | flops | bytes accessed | tf_op | source)
XLA Modules:
  0.0 125.1 jit_solution(10063901347326067936)
XLA Ops:
  0.0 1.3 %pad_add_fusion.meta = s32[8,128]{1,0:T(8,128)} fusion(s32[1,32]{1,0:T(1,128)} %param.9, s32[4,128]{1,0:T(4,128)} %bitcast.2), kind=kLoop, calls=%fused_computation | loop fusion | flops 1024 | bytes 6272 | tf_op jit(solution)/shard_map/concatenate | solution.py:454
  1.3 121.5 %lora_projection.1 = bf16[512,1024]{1,0:T(8,128)(2,1)} custom-call(bf16[512,2048]{1,0:T(8,128)(2,1)} %tokens.1, s32[8,128]{1,0:T(8,128)} %pad_add_fusion.meta, s32[256]{0:T(256)} %table.1, bf16[8192,1024]{1,0:T(8,128)(2,1)} %weight.1, bf16[8,64,2048]{2,1,0:T(8,128)(2,1)} %pool_a.1, bf16[4,128,1024]{2,1,0:T(8,128)(2,1)} %bitcast.3), custom_call_target="tpu_custom_call" | custom-call | flops 20000000000 | bytes 30000000 | tf_op jit(solution)/shard_map/lora_projection/pallas_call | solution.py:459
  122.8 2.3 %copy.9 = bf16[512,1024]{1,0:T(8,128)(2,1)} copy(bf16[512,1024]{1,0:T(8,128)(2,1)} %lora_projection.1) | data formatting | bytes 2097152

commit v3 on v2

--- a/solution.py
+++ b/solution.py
@@ -30,7 +30,7 @@
 
 
 def kernel(
-    tokens, meta, table, weight, pool_a, pool_b,
+    tokens, ids_in, list_in, table, weight, pool_a, pool_b,
     out,
     full, wts, own_tok, tok, pages_a, pb_in, pb_send, pages_b, metas, smem, pair, odds, stage,
     part_send, part_recv, mid, end, zsum, zrecv, ranks, delta_send, delta_recv, acc,
@@ -94,7 +94,9 @@
         pl.semaphore_signal(barrier, inc=1, device_id=(rep, zat(d)), device_id_type=MESH)
     for copy in (local[1], local[0], local[2], local[3], wloads[0], wloads[3], wloads[1], wloads[2]):
         copy.start()
-    metas[0] = meta[...]
+    metas[0] = jnp.zeros((8, 128), jnp.int32)
+    metas[0, 0:1, 0:32] = list_in[...]
+    metas[0, 4:8] = ids_in[...]
     pl.semaphore_wait(barrier, CHIPS - 1 + 4)
 
     def rows(c):
@@ -112,7 +114,7 @@
         return remote(part, part, z_s.at[way, 4 + n], z_r.at[way, 4 + n], dev)
 
     def send_meta(i):
-        return remote(meta, metas.at[i], m_s.at[i], m_r.at[i], (ahead(i), z))
+        return remote(metas.at[0], metas.at[i], m_s.at[i], m_r.at[i], (ahead(i), z))
 
     def send_a(i):
         to = ahead(i)
@@ -329,7 +331,7 @@
             send_rank(half, i, ahead(i)).start()
 
     def pass_ranks(half):
-        for g in range(4):
+        for g in (3, 2, 1, 0):
             for i in range(max(1, 4 * g), 4 * g + 4):
                 send_rank(half, i, rep).wait_recv()
             for d in (2, 1, 3):
@@ -376,11 +378,12 @@
         return remote(delta_send.at[i], delta_recv.at[chip], d_s.at[i], d_r.at[i], (dev, z))
 
     @pl.loop(0, CHIPS)
-    def _(i):
+    def _(step):
+        i = CHIPS - 1 - step
         for s in range(32):
             stage[s * 64 : (s + 1) * 64] = pages_b[pair[i, s]]
 
-        @pl.when(i % 4 == 0)
+        @pl.when(step % 4 == 0)
         def _():
             for half in range(2):
                 for d in range(1, 4):
@@ -450,8 +453,6 @@
 
 
 def per_device(tokens, tok_adapter, requests, owner_table, q_weight, pool_a, pool_b):
-    lists = jnp.pad(requests, ((0, 3), (0, 96)))
-    meta = jnp.concatenate([lists, tok_adapter.reshape(4, 128)], axis=0)
     dma = pltpu.SemaphoreType.DMA
     anywhere = pl.BlockSpec(memory_space=pl.ANY)
     vmem = pl.BlockSpec(memory_space=pltpu.VMEM)
@@ -459,7 +460,7 @@
     return pl.pallas_call(
         kernel,
         out_shape=jax.ShapeDtypeStruct((512, 1024), BF16),
-        in_specs=[anywhere, vmem, smem, anywhere, anywhere, anywhere],
+        in_specs=[anywhere, vmem, vmem, smem, anywhere, anywhere, anywhere],
         out_specs=vmem,
         scratch_shapes=[
             pltpu.VMEM((4, 512, 2048), BF16),
@@ -509,7 +510,7 @@
             flops=20_000_000_000, bytes_accessed=30_000_000, transcendentals=0
         ),
         name="lora_projection",
-    )(tokens, meta, owner_table, q_weight, pool_a, pool_b.reshape(4, 128, 1024))
+    )(tokens, tok_adapter.reshape(4, 128), requests, owner_table, q_weight, pool_a, pool_b.reshape(4, 128, 1024))
 
 
 def solution(mesh):

time: 125 us -> 122 us (0.976)
  Pallas kernels: 122 us -> 120 us
  other arithmetic: 1.3 us -> 0 us
    pallas_call x1, Pallas kernels: 122 us -> 120 us  [per_device(): pl.pallas_call(kernel, out_shape=jax.ShapeDtypeStruct((512, 1024), BF16),...]
    concatenate x1 -> x0, other arithmetic: 1.3 us -> none  [per_device(): meta = jnp.concatenate([lists, tok_adapter.reshape(4, 128)], axis=0)]
where the time goes in v3:
time: 122 us
  Pallas kernels  120 us (98%)
  local copies, waits for them, and re-layouts  2.26 us (2%)
    pallas_call x1, Pallas kernels, per_device(): pl.pallas_call(kernel, out_shape=jax.ShapeDtypeStruct((512, 1024), BF16),...  120 us

profile of v3, /device:TPU:0, one launch (start us, length us, event | category | flops | bytes accessed | tf_op | source)
XLA Modules:
  0.0 122.3 jit_solution(15341429982425993516)
XLA Ops:
  0.0 120.0 %lora_projection.1 = bf16[512,1024]{1,0:T(8,128)(2,1)} custom-call(bf16[512,2048]{1,0:T(8,128)(2,1)} %tokens.1, s32[4,128]{1,0:T(4,128)} %bitcast.3, s32[1,32]{1,0:T(1,128)} %list_in.1, s32[256]{0:T(256)} %table.1, bf16[8192,1024]{1,0:T(8,128)(2,1)} %weight.1, bf16[8,64,2048]{2,1,0:T(8,128)(2,1)} %pool_a.1, bf16[4,128,1024]{2,1,0:T(8,128)(2,1)} %bitcast.2), custom_call_target="tpu_custom_call" | custom-call | flops 20000000000 | bytes 30000000 | tf_op jit(solution)/shard_map/lora_projection/pallas_call | solution.py:460
  120.0 2.3 %copy.9 = bf16[512,1024]{1,0:T(8,128)(2,1)} copy(bf16[512,1024]{1,0:T(8,128)(2,1)} %lora_projection.1) | data formatting | bytes 2097152

commit v4 on v3

--- a/solution.py
+++ b/solution.py
@@ -327,7 +327,7 @@
         ranks[half, z, 0] = (
             zsum[half, z] + zrecv[half, 1] + zrecv[half, 2] + zrecv[half, 3]
         ).astype(BF16)
-        for i in range(1, CHIPS):
+        for i in range(CHIPS - 1, 0, -1):
             send_rank(half, i, ahead(i)).start()
 
     def pass_ranks(half):

time: 122 us -> 122 us (level)
  no operation moved by 1% of the time
where the time goes in v4:
time: 122 us; the launch traced here: 121 us
  Pallas kernels  119 us (98%)
  local copies, waits for them, and re-layouts  2.26 us (2%)
    pallas_call x1, Pallas kernels, per_device(): pl.pallas_call(kernel, out_shape=jax.ShapeDtypeStruct((512, 1024), BF16),...  119 us

profile of v4, /device:TPU:0, one launch (start us, length us, event | category | flops | bytes accessed | tf_op | source)
XLA Modules:
  0.0 121.5 jit_solution(13076026161031290600)
XLA Ops:
  0.0 119.2 %lora_projection.1 = bf16[512,1024]{1,0:T(8,128)(2,1)} custom-call(bf16[512,2048]{1,0:T(8,128)(2,1)} %tokens.1, s32[4,128]{1,0:T(4,128)} %bitcast.3, s32[1,32]{1,0:T(1,128)} %list_in.1, s32[256]{0:T(256)} %table.1, bf16[8192,1024]{1,0:T(8,128)(2,1)} %weight.1, bf16[8,64,2048]{2,1,0:T(8,128)(2,1)} %pool_a.1, bf16[4,128,1024]{2,1,0:T(8,128)(2,1)} %bitcast.2), custom_call_target="tpu_custom_call" | custom-call | flops 20000000000 | bytes 30000000 | tf_op jit(solution)/shard_map/lora_projection/pallas_call | solution.py:460
  119.2 2.3 %copy.9 = bf16[512,1024]{1,0:T(8,128)(2,1)} copy(bf16[512,1024]{1,0:T(8,128)(2,1)} %lora_projection.1) | data formatting | bytes 2097152
